TPU v7x, 128 devices: a whole 4x4x4 slice. The times are simulated.
128 devices in a mesh: row: 8 (over y, core), col: 16 (over x, z).
Axes of the slice: x: 4, y: 4, z: 4, core: 2. Of those that a mesh axis runs over, the one named last changes fastest.
Arguments:
- transition: bfloat16 [12288, 12288], P('row', 'col'), may hold values from 0 to 36.084392, as said below
- tile_pattern: int32 [96, 96], P('row', 'col'), may hold values from 0 to 1, as said below
- kept_tiles: int32 [96, 48], P('row', 'col'), may hold values from 0 to 1, as said below
Outputs:
- next_panel: float32 [12288, 6144], P('row', 'col')
- chaos: float32 [], replicated
Inputs may be any that keep to these rules, and one draw needn't show every extreme that they name: `tile_pattern`: each device's block of 12 x 6 tiles holds at most 36 nonzero tiles, and some block holds exactly 36. Every diagonal tile is nonzero. `kept_tiles`: for panel tile column p, the tile in tile row (p // 3) * 6 + p % 3 is always kept. `transition`: all entries are positive.
All inputs are finite; a program needn't handle non-finite values.
Results may differ from a plain program's by a relative error of at most 0.0003.
Values may be sent and summed in bfloat16 or wider, within the bound.
A program may use at most 128 MiB of HBM per device.

v0:
```python
import jax
import jax.numpy as jnp
from jax import lax
from jax.sharding import PartitionSpec as P


def expand_tiles(tile_mask, tile_size):
    return jnp.repeat(jnp.repeat(tile_mask, tile_size, axis=0), tile_size, axis=1)


def body(transition, tile_pattern, kept_tiles):
    row_tiles, col_tiles = tile_pattern.shape
    tile_size = transition.shape[0] // row_tiles
    panel_cols = kept_tiles.shape[1]
    width = panel_cols * tile_size
    masked = transition * expand_tiles(tile_pattern, tile_size).astype(jnp.bfloat16)
    own_panel = masked[:, :width]
    column_panel = lax.all_gather(own_panel, "row", axis=0, tiled=True)
    product = jnp.dot(
        lax.all_gather(masked, "col", axis=1, tiled=True),
        column_panel,
        preferred_element_type=jnp.float32,
    )
    pruned = product * expand_tiles(kept_tiles, tile_size).astype(jnp.float32)
    inflated = pruned * pruned
    col_sums, squares = lax.psum(
        (jnp.sum(inflated, axis=0), jnp.sum(inflated * inflated, axis=0)), "row"
    )
    normalized = inflated / col_sums
    spread = squares / (col_sums * col_sums)
    node_count = transition.shape[0] * lax.axis_size("row")
    col_peaks = lax.pmax(jnp.max(inflated, axis=0), "row")
    local_max = jnp.max(col_peaks / col_sums - spread)
    chaos_value = lax.pmax(local_max, "col")
    return (normalized * node_count, chaos_value * node_count)


def solution(mesh):
    placed = (P("row", "col"), P("row", "col"), P("row", "col"))
    return jax.shard_map(
        body, mesh=mesh, in_specs=placed, out_specs=(P("row", "col"), P()), check_vma=False
    )
```

profile of v0, /device:TPU:1, one launch (start us, length us, event | category | flops | bytes accessed | tf_op | source)
XLA Modules:
  0.0 391.0 jit_solution(11973173878418087578)
XLA Ops:
  7.2 0.0 all-gather.5.cloned.1.call-start
  7.2 0.7 convert_element_type.22
  7.9 0.1 broadcast_bitcast_fusion.1
  8.0 4.3 %copy.7 = bf16[1536,768]{0,1:T(8,128)(2,1)} copy(bf16[1536,768]{1,0:T(8,128)(2,1)} %param.3) | data formatting | bytes 4718592 | tf_op args[0]
  12.3 1.8 bitcast_multiply_fusion
  14.1 0.0 copy-start
  14.1 1.2 slice.4
  15.3 0.0 copy-start.1
  15.3 0.0 all-gather.5.cloned.1.call-update
  15.3 0.0 all-gather.3.cloned.1.call-start
  15.4 0.5 copy-done
  15.9 0.2 all-gather.3.cloned.1.call-update
  16.1 0.0 copy-done.1
  16.1 0.1 broadcast_bitcast_fusion
  16.2 0.3 broadcast_in_dim.16
  16.5 2.0 copy.8
  18.4 54.8 %all-gather.5.cloned.1.call-done = bf16[12288,384]{0,1:T(8,128)(2,1)} async-done(((bf16[1536,384]{0,1:T(8,128)(2,1)}), bf16[12288,384]{0,1:T(8,128)(2,1)}) %all-gather.5.cloned.1.call-update) | async-done | bytes 9437200 | tf_op jit(solution)/shard_map/all_gather | solution.py:18
  73.2 220.7 %all-gather.3.cloned.1.call-done = bf16[1536,12288]{0,1:T(8,128)(2,1)} async-done(((bf16[1536,768]{0,1:T(8,128)(2,1)}), bf16[1536,12288]{0,1:T(8,128)(2,1)}) %all-gather.3.cloned.1.call-update) | async-done | bytes 37748752 | tf_op jit(solution)/shard_map/all_gather | solution.py:20
  293.9 27.1 %fusion.1 = (f32[384]{0:T(512)S(1)}, f32[384]{0:T(512)S(1)}, f32[384]{0:T(512)S(1)}, f32[1536,384]{1,0:T(8,128)S(1)}) fusion(f32[1536,384]{1,0:T(8,128)} %copy.8, bf16[1536,12288]{0,1:T(8,128)(2,1)} %all-gather.3.cloned.1.call-done, bf16[12288,384]{0,1:T(8,128)(2,1)} %all-gather.5.cloned.1.call-done), kind=kOutput, calls=%fused_computation.10 | convolution fusion | flops 14499053568 | bytes 51909120 | tf_op jit(solution)/shard_map/dot_general | solution.py:19
  321.0 12.4 %pmax.14 = f32[384]{0:T(512)S(1)} all-reduce(f32[384]{0:T(512)S(1)} %get-tuple-element.2), channel_id=1, replica_groups=mesh['row'=8,'col'=16] {'row'}, use_global_device_ids=true, to_apply=%region_3.0 | all-reduce | flops 384 | bytes 3072 | tf_op jit(solution)/shard_map/pmax | solution.py:32
  333.4 14.6 %all-reduce = (f32[384]{0:T(512)S(1)}, f32[384]{0:T(512)S(1)}) all-reduce(f32[384]{0:T(512)S(1)} %get-tuple-element.4, f32[384]{0:T(512)S(1)} %get-tuple-element.3), channel_id=1, replica_groups=mesh['row'=8,'col'=16] {'row'}, use_global_device_ids=true, to_apply=%region_1.0 | all-reduce | flops 768 | bytes 6144 | tf_op jit(solution)/shard_map/psum | solution.py:26
  348.0 0.6 subtract_reduce_fusion
  348.6 32.1 %pmax.15 = f32[]{:T(128)} all-reduce(f32[]{:T(128)} %subtract_reduce_fusion), channel_id=1, replica_groups=mesh['row'=8,'col'=16] {'col'}, use_global_device_ids=true, to_apply=%region_7.0 | all-reduce | flops 1 | bytes 8 | tf_op jit(solution)/shard_map/pmax | solution.py:34
  380.8 1.6 divide_multiply_fusion
  (3 shorter events, 0.0 us)
Async XLA Ops:
  7.2 66.1 %all-gather.5.cloned.1.call-start = ((), (), s32[]{:S(2)}) async-start(), calls=%async_computation.1 | async-start | bytes 10616832 | tf_op jit(solution)/shard_map/all_gather | solution.py:18
  14.1 1.8 copy-start
  15.3 0.8 copy-start.1
  15.3 278.6 %all-gather.3.cloned.1.call-start = ((), (), s32[]{:S(2)}) async-start(), calls=%async_computation | async-start | bytes 40108032 | tf_op jit(solution)/shard_map/all_gather | solution.py:20
Sparse Core Ops, SparseCore 0:
  15.5 57.7 all-gather.4
  75.4 218.4 all-gather.2
where the time goes:
time: 397 us; the launch traced here: 391 us
  waiting for transfers between devices  276 us (70%)
  blocking collectives  59.2 us (15%)
  matrix products  27.1 us (7%)
  between operations  15.9 us (4%)
  local copies, waits for them, and re-layouts  8.34 us (2%)
  other arithmetic  4.71 us (1%)
    all_gather x1, waiting for transfers between devices, body(): lax.all_gather(masked, 'col', axis=1, tiled=True)  221 us
    all_gather x1, waiting for transfers between devices, body(): column_panel = lax.all_gather(own_panel, 'row', axis=0, tiled=True)  54.8 us
    pmax x1, blocking collectives, body(): chaos_value = lax.pmax(local_max, 'col')  32.1 us
    dot_general x1, matrix products, body(): jnp.dot(lax.all_gather(masked, 'col', axis=1, tiled=True), column_panel,...  27.1 us
    psum x1, blocking collectives, body(): lax.psum((jnp.sum(inflated, axis=0), jnp.sum(inflated * inflated, axis=0)...  14.6 us
    pmax x1, blocking collectives, body(): col_peaks = lax.pmax(jnp.max(inflated, axis=0), 'row')  12.4 us
  transfers between devices with their start and end apart: 2, of which 2 were waited for; matrix products, arithmetic and copies ran while one was open for 1% of the time, Pallas kernels for 0%

commit v1 on v0

v1 whole, which is shorter than its diff:
```python
import jax
import jax.numpy as jnp
from jax import lax
from jax.experimental import pallas as pl
from jax.experimental.pallas import tpu as pltpu
from jax.sharding import PartitionSpec as P

MESH = pl.DeviceIdType.MESH
T = 128
RT, KT, PT = 12, 6, 3
SLOTS = 36
HALF = 18
QUART = 9
ROWS, KW, W = RT * T, KT * T, PT * T
OFFS = [(dx, dz) for dx in range(4) for dz in range(4)]


def index_kernel(pat_ref, pos_ref, map_ref):
    def clear(s, carry):
        pos_ref[0, s] = 0
        return carry

    lax.fori_loop(0, T, clear, 0)

    def step(p, count):
        v = pat_ref[p % RT, p // RT]
        pos_ref[0, count] = p
        map_ref[0, p] = jnp.where(v > 0, count, SLOTS)
        return count + jnp.where(v > 0, 1, 0)

    lax.fori_loop(0, RT * KT, step, jnp.int32(0))


def main_kernel(pos_ref, kept_ref, map_ref, a_ref, inf_ref, stat_ref, chaos_ref, *scratch):
    bufs = dict(zip(OFFS, scratch[:16]))
    (tiles, ball, acc, dense, meta, meta_s, stats, peaks,
     loc_sem, asem_s, asem_r, bsem_s, bsem_r, msem_s, msem_r, ssem_s, ssem_r, csem_s, csem_r) = scratch[16:]
    row, col = lax.axis_index("row"), lax.axis_index("col")
    y, core = row // 2, row % 2
    x, z = col // 4, col % 4

    def plane(dx, dz):
        return (row, ((x + dx) % 4) * 4 + (z + dz) % 4)

    def line(dy, dc):
        return (((y + dy) % 4) * 2 + (core + dc) % 2, col)

    loads = [
        pltpu.make_async_copy(
            a_ref.at[:, :, pl.ds(c * T, T)], tiles.at[pl.ds(c * RT, RT)], loc_sem.at[c])
        for c in range(KT)
    ]
    for cp in loads:
        cp.start()
    own_meta = pltpu.make_async_copy(map_ref, meta.at[0], loc_sem.at[KT])
    own_meta.start()
    barrier = pltpu.get_barrier_semaphore()
    others = [plane(*o) for o in OFFS[1:]] + [line(dy, dc) for dy in range(4) for dc in range(2) if (dy, dc) != (0, 0)]
    for d in others:
        pl.semaphore_signal(barrier, inc=1, device_id=d, device_id_type=MESH)
    for o in OFFS:
        bufs[o][SLOTS] = jnp.zeros((T, T), jnp.bfloat16)
    own_meta.wait()
    for cp in loads:
        cp.wait()
    own = bufs[(0, 0)]

    def pack(s, carry):
        own[s] = tiles[pos_ref[0, s]]
        return carry

    sends = []

    def remote(src, dst, s_sem, r_sem, dev):
        cp = pltpu.make_async_remote_copy(
            src_ref=src, dst_ref=dst, send_sem=s_sem, recv_sem=r_sem, device_id=dev, device_id_type=MESH)
        cp.start()
        sends.append(cp)
        return cp

    used = {}
    acount = [0]

    def apiece(src_off, axis, sign, lo, n):
        d = [0, 0]
        d[axis] = sign
        dst_off = list(src_off)
        dst_off[axis] = (dst_off[axis] - sign) % 4
        k = acount[0]
        acount[0] += 1
        cp = remote(
            bufs[src_off].at[pl.ds(lo, n)], bufs[tuple(dst_off)].at[pl.ds(lo, n)],
            asem_s.at[k], asem_r.at[k], plane(*d))
        used[(tuple(dst_off), axis, sign, lo)] = cp

    def await_piece(off, axis, sign, lo):
        used[(off, axis, sign, lo)].wait_recv()

    def off(axis, a, b):
        return (a, b) if axis == 0 else (b, a)

    lax.fori_loop(0, SLOTS, pack, 0)
    pl.semaphore_wait(barrier, len(others))

    def spread(h, axis, o):
        apiece(o, axis, 1, h * HALF, HALF)
        apiece(o, axis, -1, h * HALF, HALF)

    def got(h, axis, o1, o3):
        await_piece(o3, axis, 1, h * HALF)
        apiece(o3, axis, 1, h * HALF, QUART)
        await_piece(o1, axis, -1, h * HALF)
        apiece(o1, axis, -1, h * HALF + QUART, QUART)

    def far(h, axis, o2):
        await_piece(o2, axis, 1, h * HALF)
        await_piece(o2, axis, -1, h * HALF + QUART)

    for h in range(2):
        spread(h, h, (0, 0))
    metas = []
    for i, o in enumerate(OFFS[1:]):
        j = OFFS[1:].index(((-o[0]) % 4, (-o[1]) % 4))
        metas.append(remote(meta.at[0], meta.at[1 + j], msem_s.at[i], msem_r.at[j], plane(*o)))
    def own_panel(r, carry):
        for c in range(PT):
            ball[pl.ds(row * ROWS + r * T, T), c * T:(c + 1) * T] = own[meta_s[0, 0, c * RT + r]]
        return carry

    cp = pltpu.make_async_copy(meta.at[0], meta_s.at[0], loc_sem.at[KT])
    cp.start()
    cp.wait()
    lax.fori_loop(0, RT, own_panel, 0)

    def bcopy(k, dy_src, core_src, lo, n, dev):
        blk = ball.at[pl.ds((((y + dy_src) % 4) * 2 + core_src) * ROWS + lo, n)]
        return remote(blk, blk, bsem_s.at[k], bsem_r.at[k], dev)

    HB = ROWS // 2
    b_up = bcopy(0, 0, core, 0, ROWS, line(1, 0))
    b_dn = bcopy(1, 0, core, 0, ROWS, line(-1, 0))
    b_sib = [bcopy(2, 0, core, 0, ROWS, line(0, 1))]
    for h in range(2):
        spread(h, 1 - h, (0, 0))
    for h in range(2):
        got(h, h, off(h, 1, 0), off(h, 3, 0))
    for h in range(2):
        spread(h, 1 - h, off(h, 1, 0))
        spread(h, 1 - h, off(h, 3, 0))
    b_up.wait_recv()
    b_up2 = bcopy(3, 3, core, 0, HB, line(1, 0))
    b_sib.append(bcopy(4, 3, core, 0, ROWS, line(0, 1)))
    b_dn.wait_recv()
    b_dn2 = bcopy(5, 1, core, HB, HB, line(-1, 0))
    b_sib.append(bcopy(6, 1, core, 0, ROWS, line(0, 1)))
    for h in range(2):
        far(h, h, off(h, 2, 0))
    for h in range(2):
        got(h, 1 - h, off(h, 0, 1), off(h, 0, 3))
    for h in range(2):
        spread(h, 1 - h, off(h, 2, 0))
    for cp in metas:
        cp.wait_recv()
    cp = pltpu.make_async_copy(meta.at[pl.ds(1, 15)], meta_s.at[pl.ds(1, 15)], loc_sem.at[KT])
    cp.start()
    cp.wait()
    b_up2.wait_recv()
    b_sib.append(bcopy(7, 2, core, 0, HB, line(0, 1)))
    b_dn2.wait_recv()
    b_sib.append(bcopy(8, 2, core, HB, HB, line(0, 1)))
    for cp in b_sib:
        cp.wait_recv()

    first = [True]

    def multiply(o):
        buf, m = bufs[o], OFFS.index(o)
        zero = first[0]
        first[0] = False
        src = ((x + o[0]) % 4) * 4 + (z + o[1]) % 4

        def expand(r, carry):
            for c in range(KT):
                dense[pl.ds(r * T, T), c * T:(c + 1) * T] = buf[meta_s[m, 0, c * RT + r]]
            return carry

        lax.fori_loop(0, RT, expand, 0)

        def mm(i, carry):
            sl = pl.ds(i * 512, 512)
            p = jnp.dot(dense[sl, :], ball[pl.ds(src * KW, KW), :], preferred_element_type=jnp.float32)
            if zero:
                acc[sl, :] = p
            else:
                acc[sl, :] += p
            return carry

        lax.fori_loop(0, ROWS // 512, mm, 0)

    for o in ((0, 0), (1, 0), (3, 0), (0, 1), (0, 3)):
        multiply(o)
    for s in (1, 3):
        for h in range(2):
            got(h, 1 - h, off(h, s, 1), off(h, s, 3))
    for h in range(2):
        far(h, 1 - h, off(h, 0, 2))
    for o in ((2, 0), (0, 2), (1, 1), (1, 3), (3, 1), (3, 3)):
        multiply(o)
    for h in range(2):
        got(h, 1 - h, off(h, 2, 1), off(h, 2, 3))
    for s in (1, 3):
        for h in range(2):
            far(h, 1 - h, off(h, s, 2))
    for o in ((1, 2), (3, 2), (2, 1), (2, 3)):
        multiply(o)
    for h in range(2):
        far(h, 1 - h, off(h, 2, 2))
    multiply((2, 2))

    sums = [jnp.zeros((8, T), jnp.float32)] * PT
    sqs = [jnp.zeros((8, T), jnp.float32)] * PT
    mxs = [jnp.zeros((8, T), jnp.float32)] * PT

    def finish(r, carry):
        out = []
        for c in range(PT):
            s, q, m = carry[c]
            sl = (pl.ds(r * T, T), slice(c * T, (c + 1) * T))
            v = acc[sl] * kept_ref[r, c].astype(jnp.float32)
            v = v * v
            acc[sl] = v
            v8 = v.reshape(T // 8, 8, T)
            out.append((s + jnp.sum(v8, axis=0), q + jnp.sum(v8 * v8, axis=0), jnp.maximum(m, jnp.max(v8, axis=0))))
        return tuple(out)

    fin = lax.fori_loop(0, RT, finish, tuple((sums[c], sqs[c], mxs[c]) for c in range(PT)))
    out_cp = pltpu.make_async_copy(acc, inf_ref, loc_sem.at[0])
    out_cp.start()
    for c in range(PT):
        s, q, m = fin[c]
        stats[row, 0:1, c * T:(c + 1) * T] = jnp.sum(s, axis=0, keepdims=True)
        stats[row, 1:2, c * T:(c + 1) * T] = jnp.sum(q, axis=0, keepdims=True)
        stats[row, 2:3, c * T:(c + 1) * T] = jnp.max(m, axis=0, keepdims=True)
    lines = [(dy, dc) for dy in range(4) for dc in range(2) if (dy, dc) != (0, 0)]
    cps = []
    for i, (dy, dc) in enumerate(lines):
        j = lines.index(((-dy) % 4, dc))
        cps.append(remote(stats.at[row], stats.at[row], ssem_s.at[i], ssem_r.at[j], line(dy, dc)))
    for cp in cps:
        cp.wait_recv()
    col_sums, squares, col_max = stats[0, 0:1, :], stats[0, 1:2, :], stats[0, 2:3, :]
    for i in range(1, 8):
        col_sums = col_sums + stats[i, 0:1, :]
        squares = squares + stats[i, 1:2, :]
        col_max = jnp.maximum(col_max, stats[i, 2:3, :])
    stat_ref[...] = jnp.broadcast_to(col_sums, (8, W))
    peak = jnp.max(col_max / col_sums - squares / (col_sums * col_sums), axis=1, keepdims=True)
    peaks[0] = jnp.broadcast_to(peak, (8, T))
    cps = []
    for i, o in enumerate(OFFS[1:]):
        j = OFFS[1:].index(((-o[0]) % 4, (-o[1]) % 4))
        cps.append(remote(peaks.at[0], peaks.at[1 + j], csem_s.at[i], csem_r.at[j], plane(*o)))
    for cp in cps:
        cp.wait_recv()
    best = peaks[0]
    for i in range(1, 16):
        best = jnp.maximum(best, peaks[i])
    chaos_ref[...] = best
    for cp in sends:
        cp.wait_send()
    out_cp.wait()


def body(transition, tile_pattern, kept_tiles):
    pos, tile_map = pl.pallas_call(
        index_kernel,
        out_shape=(jax.ShapeDtypeStruct((1, T), jnp.int32), jax.ShapeDtypeStruct((8, T), jnp.int32)),
        in_specs=[pl.BlockSpec(memory_space=pltpu.SMEM)],
        out_specs=(pl.BlockSpec(memory_space=pltpu.SMEM), pl.BlockSpec(memory_space=pltpu.SMEM)),
    )(tile_pattern)
    a = transition.reshape(RT, T, KW)
    dma = pltpu.SemaphoreType.DMA
    inflated, col_sums, chaos = pl.pallas_call(
        main_kernel,
        out_shape=(
            jax.ShapeDtypeStruct((ROWS, W), jnp.float32),
            jax.ShapeDtypeStruct((8, W), jnp.float32),
            jax.ShapeDtypeStruct((8, T), jnp.float32),
        ),
        in_specs=[
            pl.BlockSpec(memory_space=pltpu.SMEM),
            pl.BlockSpec(memory_space=pltpu.SMEM),
            pl.BlockSpec(memory_space=pl.ANY),
            pl.BlockSpec(memory_space=pl.ANY),
        ],
        out_specs=(
            pl.BlockSpec(memory_space=pl.ANY),
            pl.BlockSpec(memory_space=pltpu.VMEM),
            pl.BlockSpec(memory_space=pltpu.VMEM),
        ),
        scratch_shapes=[pltpu.VMEM((SLOTS + 1, T, T), jnp.bfloat16)] * 16
        + [
            pltpu.VMEM((RT * KT, T, T), jnp.bfloat16),
            pltpu.VMEM((8 * ROWS, W), jnp.bfloat16),
            pltpu.VMEM((ROWS, W), jnp.float32),
            pltpu.VMEM((ROWS, KW), jnp.bfloat16),
            pltpu.VMEM((16, 8, T), jnp.int32),
            pltpu.SMEM((16, 8, T), jnp.int32),
            pltpu.VMEM((8, 8, W), jnp.float32),
            pltpu.VMEM((16, 8, T), jnp.float32),
            dma((KT + 1,)),
            dma((40,)), dma((40,)),
            dma((9,)), dma((9,)),
            dma((15,)), dma((15,)),
            dma((7,)), dma((7,)),
            dma((15,)), dma((15,)),
        ],
        compiler_params=pltpu.CompilerParams(
            collective_id=0, has_side_effects=True, vmem_limit_bytes=56 * 2**20),
        cost_estimate=pl.CostEstimate(flops=14495514624, bytes_accessed=8 * 2**20, transcendentals=0),
    )(pos, kept_tiles, tile_map, a)
    node_count = transition.shape[0] * lax.axis_size("row")
    return inflated / col_sums[0] * node_count, chaos[0, 0] * node_count


def solution(mesh):
    placed = (P("row", "col"), P("row", "col"), P("row", "col"))
    return jax.shard_map(
        body, mesh=mesh, in_specs=placed, out_specs=(P("row", "col"), P()), check_vma=False
    )
```

time: 397 us -> 139 us (0.35); the launches traced: 391 us -> 138 us
  waiting for transfers between devices: 276 us -> 0 us
  Pallas kernels: 0 us -> 128 us
  blocking collectives: 59.2 us -> 0 us
  matrix products: 27.1 us -> 0 us
  between operations: 15.9 us -> 2.43 us
    all_gather x2 -> x0, waiting for transfers between devices: 275 us -> none  [the longest x1 221 us: body(): lax.all_gather(masked, 'col', axis=1, tiled=True)]
    pallas_call x0 -> x2, Pallas kernels: none -> 128 us  [the longest x1 125 us: body(): pl.pallas_call(main_kernel, out_shape=(jax.ShapeDtypeStruct((ROWS, W), jn...]
    pmax x2 -> x0, blocking collectives: 44.6 us -> none  [the longest x1 32.1 us: body(): chaos_value = lax.pmax(local_max, 'col')]
    dot_general x1 -> x0, matrix products: 27.1 us -> none  [body(): jnp.dot(lax.all_gather(masked, 'col', axis=1, tiled=True), column_panel,...]
    psum x1 -> x0, blocking collectives: 14.6 us -> none  [body(): lax.psum((jnp.sum(inflated, axis=0), jnp.sum(inflated * inflated, axis=0)...]
  transfers between devices with their start and end apart: 2 -> 0, of which waited for: 2 -> 0; matrix products, arithmetic and copies ran while one was open for 1% -> 0% of each run, Pallas kernels for 0% -> 0%
where the time goes in v1:
time: 139 us; the launch traced here: 138 us
  Pallas kernels  128 us (92%)
  local copies, waits for them, and re-layouts  4.65 us (3%)
  other arithmetic  3.24 us (2%)
  between operations  2.43 us (2%)
    pallas_call x1, Pallas kernels, body(): pl.pallas_call(main_kernel, out_shape=(jax.ShapeDtypeStruct((ROWS, W), jn...  125 us
    pallas_call x1, Pallas kernels, body(): pl.pallas_call(index_kernel, out_shape=(jax.ShapeDtypeStruct((1, T), jnp....  3.56 us
    mul x1, other arithmetic, body(): return (inflated / col_sums[0] * node_count, chaos[0, 0] * node_count)  3.24 us

profile of v1, /device:TPU:1, one launch (start us, length us, event | category | flops | bytes accessed | tf_op | source)
XLA Modules:
  0.0 138.4 jit_solution(2008844747634639357)
XLA Ops:
  0.6 1.4 copy.5.pat_ref
  2.0 3.6 %shard_map.50 = (s32[1,128]{1,0:T(1,128)}, s32[8,128]{1,0:T(8,128)}) custom-call(s32[12,6]{1,0:T(8,128)} %copy.5.pat_ref), custom_call_target="tpu_custom_call" | custom-call | tf_op jit(solution)/shard_map/pallas_call | solution.py:275
  5.6 1.4 copy.6.kept_ref
  6.9 124.5 %shard_map.51 = (f32[1536,384]{1,0:T(8,128)}, f32[8,384]{1,0:T(8,128)}, f32[8,128]{1,0:T(8,128)}) custom-call(s32[1,128]{1,0:T(1,128)} %get-tuple-element.7.pos_ref, s32[12,3]{1,0:T(8,128)} %copy.6.kept_ref, s32[8,128]{1,0:T(8,128)} %get-tuple-element.8.map_ref, bf16[12,128,768]{2,1,0:T(8,128)(2,1)} %bitcast.2), custom_call_target="tpu_custom_call" | custom-call | flops 14495514624 | bytes 8388608 | tf_op jit(solution)/shard_map/pallas_call | solution.py:283
  131.5 1.2 slice.7
  133.3 0.7 slice_reduce_fusion
  134.0 3.2 %divide_multiply_fusion = f32[1536,384]{1,0:T(8,128)} fusion(f32[1536,384]{1,0:T(8,128)} %get-tuple-element.9, f32[384]{0:T(512)S(1)} %slice_reduce_fusion), kind=kLoop, calls=%fused_computation | loop fusion | flops 1179648 | bytes 4720128 | tf_op jit(solution)/shard_map/mul | solution.py:323

commit v2 on v1

--- a/solution.py
+++ b/solution.py
@@ -15,23 +15,7 @@
 OFFS = [(dx, dz) for dx in range(4) for dz in range(4)]
 
 
-def index_kernel(pat_ref, pos_ref, map_ref):
-    def clear(s, carry):
-        pos_ref[0, s] = 0
-        return carry
-
-    lax.fori_loop(0, T, clear, 0)
-
-    def step(p, count):
-        v = pat_ref[p % RT, p // RT]
-        pos_ref[0, count] = p
-        map_ref[0, p] = jnp.where(v > 0, count, SLOTS)
-        return count + jnp.where(v > 0, 1, 0)
-
-    lax.fori_loop(0, RT * KT, step, jnp.int32(0))
-
-
-def main_kernel(pos_ref, kept_ref, map_ref, a_ref, inf_ref, stat_ref, chaos_ref, *scratch):
+def main_kernel(pat_ref, kept_ref, a_ref, out_ref, chaos_ref, *scratch):
     bufs = dict(zip(OFFS, scratch[:16]))
     (tiles, ball, acc, dense, meta, meta_s, stats, peaks,
      loc_sem, asem_s, asem_r, bsem_s, bsem_r, msem_s, msem_r, ssem_s, ssem_r, csem_s, csem_r) = scratch[16:]
@@ -52,12 +36,33 @@
     ]
     for cp in loads:
         cp.start()
-    own_meta = pltpu.make_async_copy(map_ref, meta.at[0], loc_sem.at[KT])
-    own_meta.start()
     barrier = pltpu.get_barrier_semaphore()
     others = [plane(*o) for o in OFFS[1:]] + [line(dy, dc) for dy in range(4) for dc in range(2) if (dy, dc) != (0, 0)]
     for d in others:
         pl.semaphore_signal(barrier, inc=1, device_id=d, device_id_type=MESH)
+
+    pat = pat_ref[...]
+    lane = lax.broadcasted_iota(jnp.int32, (KT, T), 1)
+    run = jnp.zeros((1, RT), jnp.int32)
+    below = []
+    for c in range(KT):
+        run = run + pat[c:c + 1, :]
+        below.append(run)
+    count = jnp.concatenate(below, axis=0)
+    for r in range(RT - 1):
+        count = count + jnp.where(lane[:, :RT] > r, run[:, r:r + 1], 0)
+    ends = jnp.zeros((KT, T), jnp.int32)
+    for r in range(RT):
+        ends = ends + jnp.where(count[:, r:r + 1] <= lane, 1, 0)
+    pos = ends[0:1, :]
+    for c in range(1, KT):
+        pos = pos + ends[c:c + 1, :]
+    meta[0] = jnp.zeros((16, T), jnp.int32)
+    meta[0, 0:KT, 0:RT] = jnp.where(pat > 0, count - 1, SLOTS)
+    meta[0, KT:KT + 1, :] = jnp.minimum(pos, RT * KT - 1)
+    meta[0, 8:8 + PT, 0:RT] = kept_ref[...]
+    own_meta = pltpu.make_async_copy(meta.at[0], meta_s.at[0], loc_sem.at[KT])
+    own_meta.start()
     for o in OFFS:
         bufs[o][SLOTS] = jnp.zeros((T, T), jnp.bfloat16)
     own_meta.wait()
@@ -66,7 +71,8 @@
     own = bufs[(0, 0)]
 
     def pack(s, carry):
-        own[s] = tiles[pos_ref[0, s]]
+        p = meta_s[0, KT, s]
+        own[s] = tiles[p % KT * RT + p // KT]
         return carry
 
     sends = []
@@ -124,12 +130,9 @@
         metas.append(remote(meta.at[0], meta.at[1 + j], msem_s.at[i], msem_r.at[j], plane(*o)))
     def own_panel(r, carry):
         for c in range(PT):
-            ball[pl.ds(row * ROWS + r * T, T), c * T:(c + 1) * T] = own[meta_s[0, 0, c * RT + r]]
+            ball[pl.ds(row * ROWS + r * T, T), c * T:(c + 1) * T] = own[meta_s[0, c, r]]
         return carry
 
-    cp = pltpu.make_async_copy(meta.at[0], meta_s.at[0], loc_sem.at[KT])
-    cp.start()
-    cp.wait()
     lax.fori_loop(0, RT, own_panel, 0)
 
     def bcopy(k, dy_src, core_src, lo, n, dev):
@@ -179,23 +182,14 @@
         first[0] = False
         src = ((x + o[0]) % 4) * 4 + (z + o[1]) % 4
 
-        def expand(r, carry):
+        for r in range(RT):
             for c in range(KT):
-                dense[pl.ds(r * T, T), c * T:(c + 1) * T] = buf[meta_s[m, 0, c * RT + r]]
-            return carry
-
-        lax.fori_loop(0, RT, expand, 0)
-
-        def mm(i, carry):
-            sl = pl.ds(i * 512, 512)
-            p = jnp.dot(dense[sl, :], ball[pl.ds(src * KW, KW), :], preferred_element_type=jnp.float32)
-            if zero:
-                acc[sl, :] = p
-            else:
-                acc[sl, :] += p
-            return carry
-
-        lax.fori_loop(0, ROWS // 512, mm, 0)
+                dense[r * T:(r + 1) * T, c * T:(c + 1) * T] = buf[meta_s[m, c, r]]
+        p = jnp.dot(dense[...], ball[pl.ds(src * KW, KW), :], preferred_element_type=jnp.float32)
+        if zero:
+            acc[...] = p
+        else:
+            acc[...] += p
 
     for o in ((0, 0), (1, 0), (3, 0), (0, 1), (0, 3)):
         multiply(o)
@@ -226,7 +220,7 @@
         for c in range(PT):
             s, q, m = carry[c]
             sl = (pl.ds(r * T, T), slice(c * T, (c + 1) * T))
-            v = acc[sl] * kept_ref[r, c].astype(jnp.float32)
+            v = acc[sl] * meta_s[0, 8 + c, r].astype(jnp.float32)
             v = v * v
             acc[sl] = v
             v8 = v.reshape(T // 8, 8, T)
@@ -234,8 +228,6 @@
         return tuple(out)
 
     fin = lax.fori_loop(0, RT, finish, tuple((sums[c], sqs[c], mxs[c]) for c in range(PT)))
-    out_cp = pltpu.make_async_copy(acc, inf_ref, loc_sem.at[0])
-    out_cp.start()
     for c in range(PT):
         s, q, m = fin[c]
         stats[row, 0:1, c * T:(c + 1) * T] = jnp.sum(s, axis=0, keepdims=True)
@@ -253,50 +245,49 @@
         col_sums = col_sums + stats[i, 0:1, :]
         squares = squares + stats[i, 1:2, :]
         col_max = jnp.maximum(col_max, stats[i, 2:3, :])
-    stat_ref[...] = jnp.broadcast_to(col_sums, (8, W))
     peak = jnp.max(col_max / col_sums - squares / (col_sums * col_sums), axis=1, keepdims=True)
     peaks[0] = jnp.broadcast_to(peak, (8, T))
     cps = []
     for i, o in enumerate(OFFS[1:]):
         j = OFFS[1:].index(((-o[0]) % 4, (-o[1]) % 4))
         cps.append(remote(peaks.at[0], peaks.at[1 + j], csem_s.at[i], csem_r.at[j], plane(*o)))
+    inverse = 1.0 / col_sums
+    nodes = float(8 * ROWS)
+    out_cps = []
+    for i in range(4):
+        sl = pl.ds(i * (ROWS // 4), ROWS // 4)
+        acc[sl, :] = acc[sl, :] * inverse * nodes
+        out_cps.append(pltpu.make_async_copy(acc.at[sl], out_ref.at[sl], loc_sem.at[i]))
+        out_cps[-1].start()
     for cp in cps:
         cp.wait_recv()
     best = peaks[0]
     for i in range(1, 16):
         best = jnp.maximum(best, peaks[i])
-    chaos_ref[...] = best
+    chaos_ref[0, 0] = jnp.max(best) * nodes
     for cp in sends:
         cp.wait_send()
-    out_cp.wait()
+    for cp in out_cps:
+        cp.wait()
 
 
 def body(transition, tile_pattern, kept_tiles):
-    pos, tile_map = pl.pallas_call(
-        index_kernel,
-        out_shape=(jax.ShapeDtypeStruct((1, T), jnp.int32), jax.ShapeDtypeStruct((8, T), jnp.int32)),
-        in_specs=[pl.BlockSpec(memory_space=pltpu.SMEM)],
-        out_specs=(pl.BlockSpec(memory_space=pltpu.SMEM), pl.BlockSpec(memory_space=pltpu.SMEM)),
-    )(tile_pattern)
     a = transition.reshape(RT, T, KW)
     dma = pltpu.SemaphoreType.DMA
-    inflated, col_sums, chaos = pl.pallas_call(
+    panel, chaos = pl.pallas_call(
         main_kernel,
         out_shape=(
             jax.ShapeDtypeStruct((ROWS, W), jnp.float32),
-            jax.ShapeDtypeStruct((8, W), jnp.float32),
-            jax.ShapeDtypeStruct((8, T), jnp.float32),
+            jax.ShapeDtypeStruct((1, 1), jnp.float32),
         ),
         in_specs=[
-            pl.BlockSpec(memory_space=pltpu.SMEM),
-            pl.BlockSpec(memory_space=pltpu.SMEM),
-            pl.BlockSpec(memory_space=pl.ANY),
+            pl.BlockSpec(memory_space=pltpu.VMEM),
+            pl.BlockSpec(memory_space=pltpu.VMEM),
             pl.BlockSpec(memory_space=pl.ANY),
         ],
         out_specs=(
             pl.BlockSpec(memory_space=pl.ANY),
-            pl.BlockSpec(memory_space=pltpu.VMEM),
-            pl.BlockSpec(memory_space=pltpu.VMEM),
+            pl.BlockSpec(memory_space=pltpu.SMEM),
         ),
         scratch_shapes=[pltpu.VMEM((SLOTS + 1, T, T), jnp.bfloat16)] * 16
         + [
@@ -304,8 +295,8 @@
             pltpu.VMEM((8 * ROWS, W), jnp.bfloat16),
             pltpu.VMEM((ROWS, W), jnp.float32),
             pltpu.VMEM((ROWS, KW), jnp.bfloat16),
-            pltpu.VMEM((16, 8, T), jnp.int32),
-            pltpu.SMEM((16, 8, T), jnp.int32),
+            pltpu.VMEM((16, 16, T), jnp.int32),
+            pltpu.SMEM((16, 16, T), jnp.int32),
             pltpu.VMEM((8, 8, W), jnp.float32),
             pltpu.VMEM((16, 8, T), jnp.float32),
             dma((KT + 1,)),
@@ -318,9 +309,8 @@
         compiler_params=pltpu.CompilerParams(
             collective_id=0, has_side_effects=True, vmem_limit_bytes=56 * 2**20),
         cost_estimate=pl.CostEstimate(flops=14495514624, bytes_accessed=8 * 2**20, transcendentals=0),
-    )(pos, kept_tiles, tile_map, a)
-    node_count = transition.shape[0] * lax.axis_size("row")
-    return inflated / col_sums[0] * node_count, chaos[0, 0] * node_count
+    )(tile_pattern.T, kept_tiles.T, a)
+    return panel, chaos.reshape(())
 
 
 def solution(mesh):

time: 139 us -> 126 us (0.906)
  Pallas kernels: 128 us -> 120 us
  other arithmetic: 3.24 us -> 0 us
  local copies, waits for them, and re-layouts: 4.65 us -> 3.22 us
    pallas_call x1, Pallas kernels: 125 us -> 120 us  [body(): pl.pallas_call(main_kernel, out_shape=(jax.ShapeDtypeStruct((ROWS, W), jn...]
    pallas_call x1 -> x0, Pallas kernels: 3.56 us -> none  [body(): pl.pallas_call(index_kernel, out_shape=(jax.ShapeDtypeStruct((1, T), jnp....]
    mul x1 -> x0, other arithmetic: 3.24 us -> none  [body(): return (inflated / col_sums[0] * node_count, chaos[0, 0] * node_count)]
    slice x2 -> x0, local copies, waits for them, and re-layouts: 1.92 us -> none  [body(): return (inflated / col_sums[0] * node_count, chaos[0, 0] * node_count)]
    unnamed x2 -> x1, local copies, waits for them, and re-layouts: 2.73 us -> 3.22 us
where the time goes in v2:
time: 126 us
  Pallas kernels  120 us (95%)
  local copies, waits for them, and re-layouts  3.22 us (3%)
  between operations  2.39 us (2%)
    pallas_call x1, Pallas kernels, body(): pl.pallas_call(main_kernel, out_shape=(jax.ShapeDtypeStruct((ROWS, W), jn...  120 us
    unnamed x1, local copies, waits for them, and re-layouts  3.22 us

profile of v2, /device:TPU:1, one launch (start us, length us, event | category | flops | bytes accessed | tf_op | source)
XLA Modules:
  0.0 126.0 jit_solution(3166720377186760224)
XLA Ops:
  0.6 120.4 %shard_map.50 = (f32[1536,384]{1,0:T(8,128)}, f32[1,1]{1,0:T(1,128)}) custom-call(s32[6,12]{1,0:T(8,128)} %bitcast.5, s32[3,12]{1,0:T(4,128)} %bitcast.6, bf16[12,128,768]{2,1,0:T(8,128)(2,1)} %bitcast.4), custom_call_target="tpu_custom_call" | custom-call | flops 14495514624 | bytes 8388608 | tf_op jit(solution)/shard_map/pallas_call | solution.py:277
  121.0 3.2 %copy.7 = f32[1536,384]{1,0:T(8,128)} copy(f32[1536,384]{1,0:T(8,128)} %get-tuple-element.8) | data formatting | bytes 4718592

commit v3 on v2

--- a/solution.py
+++ b/solution.py
@@ -17,7 +17,7 @@
 
 def main_kernel(pat_ref, kept_ref, a_ref, out_ref, chaos_ref, *scratch):
     bufs = dict(zip(OFFS, scratch[:16]))
-    (tiles, ball, acc, dense, meta, meta_s, stats, peaks,
+    (tiles, ball, acc, dense, meta, meta_s, stats, peaks, pat_v, kept_v,
      loc_sem, asem_s, asem_r, bsem_s, bsem_r, msem_s, msem_r, ssem_s, ssem_r, csem_s, csem_r) = scratch[16:]
     row, col = lax.axis_index("row"), lax.axis_index("col")
     y, core = row // 2, row % 2
@@ -29,19 +29,27 @@
     def line(dy, dc):
         return (((y + dy) % 4) * 2 + (core + dc) % 2, col)
 
+    barrier = pltpu.get_barrier_semaphore()
+    others = [plane(*o) for o in OFFS[1:]] + [line(dy, dc) for dy in range(4) for dc in range(2) if (dy, dc) != (0, 0)]
+    for d in others:
+        pl.semaphore_signal(barrier, inc=1, device_id=d, device_id_type=MESH)
+    small = [
+        pltpu.make_async_copy(pat_ref, pat_v, loc_sem.at[KT]),
+        pltpu.make_async_copy(kept_ref, kept_v, loc_sem.at[KT + 1]),
+    ]
     loads = [
         pltpu.make_async_copy(
             a_ref.at[:, :, pl.ds(c * T, T)], tiles.at[pl.ds(c * RT, RT)], loc_sem.at[c])
         for c in range(KT)
     ]
-    for cp in loads:
+    for cp in small + loads:
         cp.start()
-    barrier = pltpu.get_barrier_semaphore()
-    others = [plane(*o) for o in OFFS[1:]] + [line(dy, dc) for dy in range(4) for dc in range(2) if (dy, dc) != (0, 0)]
-    for d in others:
-        pl.semaphore_signal(barrier, inc=1, device_id=d, device_id_type=MESH)
-
-    pat = pat_ref[...]
+    for o in OFFS:
+        bufs[o][SLOTS] = jnp.zeros((T, T), jnp.bfloat16)
+    for cp in small:
+        cp.wait()
+
+    pat = pat_v[...]
     lane = lax.broadcasted_iota(jnp.int32, (KT, T), 1)
     run = jnp.zeros((1, RT), jnp.int32)
     below = []
@@ -60,11 +68,9 @@
     meta[0] = jnp.zeros((16, T), jnp.int32)
     meta[0, 0:KT, 0:RT] = jnp.where(pat > 0, count - 1, SLOTS)
     meta[0, KT:KT + 1, :] = jnp.minimum(pos, RT * KT - 1)
-    meta[0, 8:8 + PT, 0:RT] = kept_ref[...]
+    meta[0, 8:8 + PT, 0:RT] = kept_v[...]
     own_meta = pltpu.make_async_copy(meta.at[0], meta_s.at[0], loc_sem.at[KT])
     own_meta.start()
-    for o in OFFS:
-        bufs[o][SLOTS] = jnp.zeros((T, T), jnp.bfloat16)
     own_meta.wait()
     for cp in loads:
         cp.wait()
@@ -122,12 +128,13 @@
         await_piece(o2, axis, 1, h * HALF)
         await_piece(o2, axis, -1, h * HALF + QUART)
 
+    def mcopy(k, lo, n, to, dev):
+        return remote(meta.at[pl.ds(lo, n)], meta.at[pl.ds(to, n)], msem_s.at[k], msem_r.at[k], dev)
+
+    m_x = [mcopy(0, 0, 1, 3, plane(1, 0)), mcopy(1, 0, 1, 1, plane(3, 0))]
+
     for h in range(2):
         spread(h, h, (0, 0))
-    metas = []
-    for i, o in enumerate(OFFS[1:]):
-        j = OFFS[1:].index(((-o[0]) % 4, (-o[1]) % 4))
-        metas.append(remote(meta.at[0], meta.at[1 + j], msem_s.at[i], msem_r.at[j], plane(*o)))
     def own_panel(r, carry):
         for c in range(PT):
             ball[pl.ds(row * ROWS + r * T, T), c * T:(c + 1) * T] = own[meta_s[0, c, r]]
@@ -145,8 +152,13 @@
     b_sib = [bcopy(2, 0, core, 0, ROWS, line(0, 1))]
     for h in range(2):
         spread(h, 1 - h, (0, 0))
+    for cp in m_x:
+        cp.wait_recv()
+    m_x2 = mcopy(2, 3, 1, 2, plane(1, 0))
     for h in range(2):
         got(h, h, off(h, 1, 0), off(h, 3, 0))
+    m_x2.wait_recv()
+    m_z = [mcopy(3, 0, 4, 12, plane(0, 1)), mcopy(4, 0, 4, 4, plane(0, 3))]
     for h in range(2):
         spread(h, 1 - h, off(h, 1, 0))
         spread(h, 1 - h, off(h, 3, 0))
@@ -162,11 +174,17 @@
         got(h, 1 - h, off(h, 0, 1), off(h, 0, 3))
     for h in range(2):
         spread(h, 1 - h, off(h, 2, 0))
-    for cp in metas:
-        cp.wait_recv()
-    cp = pltpu.make_async_copy(meta.at[pl.ds(1, 15)], meta_s.at[pl.ds(1, 15)], loc_sem.at[KT])
-    cp.start()
-    cp.wait()
+    for cp in m_z:
+        cp.wait_recv()
+    m_z2 = mcopy(5, 12, 4, 8, plane(0, 1))
+
+    def fetch_maps(lo):
+        cp = pltpu.make_async_copy(meta.at[pl.ds(lo, 4)], meta_s.at[pl.ds(lo, 4)], loc_sem.at[KT])
+        cp.start()
+        cp.wait()
+
+    for lo in (0, 4, 12):
+        fetch_maps(lo)
     b_up2.wait_recv()
     b_sib.append(bcopy(7, 2, core, 0, HB, line(0, 1)))
     b_dn2.wait_recv()
@@ -177,7 +195,7 @@
     first = [True]
 
     def multiply(o):
-        buf, m = bufs[o], OFFS.index(o)
+        buf, m = bufs[o], o[1] * 4 + o[0]
         zero = first[0]
         first[0] = False
         src = ((x + o[0]) % 4) * 4 + (z + o[1]) % 4
@@ -198,6 +216,8 @@
             got(h, 1 - h, off(h, s, 1), off(h, s, 3))
     for h in range(2):
         far(h, 1 - h, off(h, 0, 2))
+    m_z2.wait_recv()
+    fetch_maps(8)
     for o in ((2, 0), (0, 2), (1, 1), (1, 3), (3, 1), (3, 3)):
         multiply(o)
     for h in range(2):
@@ -253,12 +273,7 @@
         cps.append(remote(peaks.at[0], peaks.at[1 + j], csem_s.at[i], csem_r.at[j], plane(*o)))
     inverse = 1.0 / col_sums
     nodes = float(8 * ROWS)
-    out_cps = []
-    for i in range(4):
-        sl = pl.ds(i * (ROWS // 4), ROWS // 4)
-        acc[sl, :] = acc[sl, :] * inverse * nodes
-        out_cps.append(pltpu.make_async_copy(acc.at[sl], out_ref.at[sl], loc_sem.at[i]))
-        out_cps[-1].start()
+    out_ref[...] = acc[...] * inverse * nodes
     for cp in cps:
         cp.wait_recv()
     best = peaks[0]
@@ -267,8 +282,6 @@
     chaos_ref[0, 0] = jnp.max(best) * nodes
     for cp in sends:
         cp.wait_send()
-    for cp in out_cps:
-        cp.wait()
 
 
 def body(transition, tile_pattern, kept_tiles):
@@ -281,12 +294,12 @@
             jax.ShapeDtypeStruct((1, 1), jnp.float32),
         ),
         in_specs=[
-            pl.BlockSpec(memory_space=pltpu.VMEM),
-            pl.BlockSpec(memory_space=pltpu.VMEM),
-            pl.BlockSpec(memory_space=pl.ANY),
+            pl.BlockSpec(memory_space=pltpu.HBM),
+            pl.BlockSpec(memory_space=pltpu.HBM),
+            pl.BlockSpec(memory_space=pltpu.HBM),
         ],
         out_specs=(
-            pl.BlockSpec(memory_space=pl.ANY),
+            pl.BlockSpec(memory_space=pltpu.VMEM),
             pl.BlockSpec(memory_space=pltpu.SMEM),
         ),
         scratch_shapes=[pltpu.VMEM((SLOTS + 1, T, T), jnp.bfloat16)] * 16
@@ -299,15 +312,17 @@
             pltpu.SMEM((16, 16, T), jnp.int32),
             pltpu.VMEM((8, 8, W), jnp.float32),
             pltpu.VMEM((16, 8, T), jnp.float32),
-            dma((KT + 1,)),
+            pltpu.VMEM((KT, RT), jnp.int32),
+            pltpu.VMEM((PT, RT), jnp.int32),
+            dma((KT + 2,)),
             dma((40,)), dma((40,)),
             dma((9,)), dma((9,)),
-            dma((15,)), dma((15,)),
+            dma((6,)), dma((6,)),
             dma((7,)), dma((7,)),
             dma((15,)), dma((15,)),
         ],
         compiler_params=pltpu.CompilerParams(
-            collective_id=0, has_side_effects=True, vmem_limit_bytes=56 * 2**20),
+            collective_id=0, has_side_effects=True, vmem_limit_bytes=50 * 2**20),
         cost_estimate=pl.CostEstimate(flops=14495514624, bytes_accessed=8 * 2**20, transcendentals=0),
     )(tile_pattern.T, kept_tiles.T, a)
     return panel, chaos.reshape(())

time: 126 us -> 124 us (0.984)
    pallas_call x1, Pallas kernels: 120 us -> 119 us  [body(): pl.pallas_call(main_kernel, out_shape=(jax.ShapeDtypeStruct((ROWS, W), jn...]
    unnamed x1 -> x5, local copies, waits for them, and re-layouts: 3.22 us -> 2.77 us
where the time goes in v3:
time: 124 us
  Pallas kernels  119 us (96%)
  local copies, waits for them, and re-layouts  2.77 us (2%)
  between operations  2.41 us (2%)
    pallas_call x1, Pallas kernels, body(): pl.pallas_call(main_kernel, out_shape=(jax.ShapeDtypeStruct((ROWS, W), jn...  119 us
    unnamed x5, local copies, waits for them, and re-layouts  2.77 us

profile of v3, /device:TPU:1, one launch (start us, length us, event | category | flops | bytes accessed | tf_op | source)
XLA Modules:
  0.0 124.0 jit_solution(10862043786190961773)
XLA Ops:
  0.6 0.0 copy-start
  0.6 0.7 copy-done
  1.3 0.0 copy-start.1
  1.3 0.7 copy-done.1
  2.0 118.8 %shard_map.50 = (f32[1536,384]{1,0:T(8,128)S(1)}, f32[1,1]{1,0:T(1,128)}) custom-call(s32[6,12]{1,0:T(8,128)S(1)} %bitcast.4, s32[3,12]{1,0:T(4,128)S(1)} %bitcast.5, bf16[12,128,768]{2,1,0:T(8,128)(2,1)} %bitcast.6), custom_call_target="tpu_custom_call" | custom-call | flops 14495514624 | bytes 8388608 | tf_op jit(solution)/shard_map/pallas_call | solution.py:290
  120.8 1.4 %copy.7 = f32[1536,384]{1,0:T(8,128)} copy(f32[1536,384]{1,0:T(8,128)S(1)} %get-tuple-element.8) | data formatting | bytes 4718592
Async XLA Ops:
  0.6 0.7 copy-start
  1.3 0.7 copy-start.1

commit v4 on v3

--- a/solution.py
+++ b/solution.py
@@ -17,7 +17,7 @@
 
 def main_kernel(pat_ref, kept_ref, a_ref, out_ref, chaos_ref, *scratch):
     bufs = dict(zip(OFFS, scratch[:16]))
-    (tiles, ball, acc, dense, meta, meta_s, stats, peaks, pat_v, kept_v,
+    (tiles, ball, acc, dense, meta, meta_s, stats, peaks,
      loc_sem, asem_s, asem_r, bsem_s, bsem_r, msem_s, msem_r, ssem_s, ssem_r, csem_s, csem_r) = scratch[16:]
     row, col = lax.axis_index("row"), lax.axis_index("col")
     y, core = row // 2, row % 2
@@ -33,44 +33,31 @@
     others = [plane(*o) for o in OFFS[1:]] + [line(dy, dc) for dy in range(4) for dc in range(2) if (dy, dc) != (0, 0)]
     for d in others:
         pl.semaphore_signal(barrier, inc=1, device_id=d, device_id_type=MESH)
-    small = [
-        pltpu.make_async_copy(pat_ref, pat_v, loc_sem.at[KT]),
-        pltpu.make_async_copy(kept_ref, kept_v, loc_sem.at[KT + 1]),
-    ]
     loads = [
         pltpu.make_async_copy(
             a_ref.at[:, :, pl.ds(c * T, T)], tiles.at[pl.ds(c * RT, RT)], loc_sem.at[c])
         for c in range(KT)
     ]
-    for cp in small + loads:
+    for cp in loads:
         cp.start()
+    lane = lax.broadcasted_iota(jnp.int32, (1, T), 1)
+    count = jnp.int32(0)
+    pos = jnp.zeros((1, T), jnp.int32)
+    maps = [pos] * KT
+    for r in range(RT):
+        for c in range(KT):
+            v = pat_ref[c, r]
+            maps[c] = jnp.where(lane == r, jnp.where(v > 0, count, SLOTS), maps[c])
+            count = count + v
+            pos = pos + jnp.where(count <= lane, 1, 0)
+    for c in range(KT):
+        meta[0, c:c + 1, :] = maps[c]
+    meta[0, KT:KT + 1, :] = jnp.minimum(pos, RT * KT - 1)
+    meta[0, KT + 1:8, :] = jnp.zeros((1, T), jnp.int32)
+    own_meta = pltpu.make_async_copy(meta.at[0], meta_s.at[0], loc_sem.at[KT])
+    own_meta.start()
     for o in OFFS:
         bufs[o][SLOTS] = jnp.zeros((T, T), jnp.bfloat16)
-    for cp in small:
-        cp.wait()
-
-    pat = pat_v[...]
-    lane = lax.broadcasted_iota(jnp.int32, (KT, T), 1)
-    run = jnp.zeros((1, RT), jnp.int32)
-    below = []
-    for c in range(KT):
-        run = run + pat[c:c + 1, :]
-        below.append(run)
-    count = jnp.concatenate(below, axis=0)
-    for r in range(RT - 1):
-        count = count + jnp.where(lane[:, :RT] > r, run[:, r:r + 1], 0)
-    ends = jnp.zeros((KT, T), jnp.int32)
-    for r in range(RT):
-        ends = ends + jnp.where(count[:, r:r + 1] <= lane, 1, 0)
-    pos = ends[0:1, :]
-    for c in range(1, KT):
-        pos = pos + ends[c:c + 1, :]
-    meta[0] = jnp.zeros((16, T), jnp.int32)
-    meta[0, 0:KT, 0:RT] = jnp.where(pat > 0, count - 1, SLOTS)
-    meta[0, KT:KT + 1, :] = jnp.minimum(pos, RT * KT - 1)
-    meta[0, 8:8 + PT, 0:RT] = kept_v[...]
-    own_meta = pltpu.make_async_copy(meta.at[0], meta_s.at[0], loc_sem.at[KT])
-    own_meta.start()
     own_meta.wait()
     for cp in loads:
         cp.wait()
@@ -111,7 +98,7 @@
     def off(axis, a, b):
         return (a, b) if axis == 0 else (b, a)
 
-    lax.fori_loop(0, SLOTS, pack, 0)
+    lax.fori_loop(0, HALF, pack, 0)
     pl.semaphore_wait(barrier, len(others))
 
     def spread(h, axis, o):
@@ -133,8 +120,9 @@
 
     m_x = [mcopy(0, 0, 1, 3, plane(1, 0)), mcopy(1, 0, 1, 1, plane(3, 0))]
 
-    for h in range(2):
-        spread(h, h, (0, 0))
+    spread(0, 0, (0, 0))
+    lax.fori_loop(HALF, SLOTS, pack, 0)
+    spread(1, 1, (0, 0))
     def own_panel(r, carry):
         for c in range(PT):
             ball[pl.ds(row * ROWS + r * T, T), c * T:(c + 1) * T] = own[meta_s[0, c, r]]
@@ -240,7 +228,7 @@
         for c in range(PT):
             s, q, m = carry[c]
             sl = (pl.ds(r * T, T), slice(c * T, (c + 1) * T))
-            v = acc[sl] * meta_s[0, 8 + c, r].astype(jnp.float32)
+            v = acc[sl] * kept_ref[c, r].astype(jnp.float32)
             v = v * v
             acc[sl] = v
             v8 = v.reshape(T // 8, 8, T)
@@ -294,8 +282,8 @@
             jax.ShapeDtypeStruct((1, 1), jnp.float32),
         ),
         in_specs=[
-            pl.BlockSpec(memory_space=pltpu.HBM),
-            pl.BlockSpec(memory_space=pltpu.HBM),
+            pl.BlockSpec(memory_space=pltpu.SMEM),
+            pl.BlockSpec(memory_space=pltpu.SMEM),
             pl.BlockSpec(memory_space=pltpu.HBM),
         ],
         out_specs=(
@@ -308,13 +296,11 @@
             pltpu.VMEM((8 * ROWS, W), jnp.bfloat16),
             pltpu.VMEM((ROWS, W), jnp.float32),
             pltpu.VMEM((ROWS, KW), jnp.bfloat16),
-            pltpu.VMEM((16, 16, T), jnp.int32),
-            pltpu.SMEM((16, 16, T), jnp.int32),
+            pltpu.VMEM((16, 8, T), jnp.int32),
+            pltpu.SMEM((16, 8, T), jnp.int32),
             pltpu.VMEM((8, 8, W), jnp.float32),
             pltpu.VMEM((16, 8, T), jnp.float32),
-            pltpu.VMEM((KT, RT), jnp.int32),
-            pltpu.VMEM((PT, RT), jnp.int32),
-            dma((KT + 2,)),
+            dma((KT + 1,)),
             dma((40,)), dma((40,)),
             dma((9,)), dma((9,)),
             dma((6,)), dma((6,)),
@@ -324,7 +310,7 @@
         compiler_params=pltpu.CompilerParams(
             collective_id=0, has_side_effects=True, vmem_limit_bytes=50 * 2**20),
         cost_estimate=pl.CostEstimate(flops=14495514624, bytes_accessed=8 * 2**20, transcendentals=0),
-    )(tile_pattern.T, kept_tiles.T, a)
+    )(*(pltpu.with_memory_space_constraint(v, pltpu.HBM) for v in (tile_pattern.T, kept_tiles.T, a)))
     return panel, chaos.reshape(())
 
 

time: 124 us -> 123 us (level)
  local copies, waits for them, and re-layouts: 2.77 us -> 1.41 us
    unnamed x5 -> x1, local copies, waits for them, and re-layouts: 2.77 us -> 1.41 us
where the time goes in v4:
time: 123 us
  Pallas kernels  119 us (97%)
  between operations  2.33 us (2%)
  local copies, waits for them, and re-layouts  1.41 us (1%)
    pallas_call x1, Pallas kernels, body(): pl.pallas_call(main_kernel, out_shape=(jax.ShapeDtypeStruct((ROWS, W), jn...  119 us

profile of v4, /device:TPU:1, one launch (start us, length us, event | category | flops | bytes accessed | tf_op | source)
XLA Modules:
  0.0 122.8 jit_solution(8505909685557432216)
XLA Ops:
  0.6 119.1 %shard_map.50 = (f32[1536,384]{1,0:T(8,128)S(1)}, f32[1,1]{1,0:T(1,128)}) custom-call(s32[6,12]{1,0:T(8,128)} %bitcast.5, s32[3,12]{1,0:T(4,128)} %bitcast.6, bf16[12,128,768]{2,1,0:T(8,128)(2,1)} %bitcast.4), custom_call_target="tpu_custom_call" | custom-call | flops 14495514624 | bytes 8388608 | tf_op jit(solution)/shard_map/pallas_call | solution.py:278
  119.7 1.4 %copy.7 = f32[1536,384]{1,0:T(8,128)} copy(f32[1536,384]{1,0:T(8,128)S(1)} %get-tuple-element.8) | data formatting | bytes 4718592

commit v5 on v4

--- a/solution.py
+++ b/solution.py
@@ -30,7 +30,8 @@
         return (((y + dy) % 4) * 2 + (core + dc) % 2, col)
 
     barrier = pltpu.get_barrier_semaphore()
-    others = [plane(*o) for o in OFFS[1:]] + [line(dy, dc) for dy in range(4) for dc in range(2) if (dy, dc) != (0, 0)]
+    others = [plane(*o) for o in sorted(OFFS[1:], key=lambda o: min(o[0], 4 - o[0]) + min(o[1], 4 - o[1]))]
+    others += [line(dy, dc) for dy in range(4) for dc in range(2) if (dy, dc) != (0, 0)]
     for d in others:
         pl.semaphore_signal(barrier, inc=1, device_id=d, device_id_type=MESH)
     loads = [
@@ -206,15 +207,17 @@
         far(h, 1 - h, off(h, 0, 2))
     m_z2.wait_recv()
     fetch_maps(8)
-    for o in ((2, 0), (0, 2), (1, 1), (1, 3), (3, 1), (3, 3)):
+    for o in ((2, 0), (0, 2), (1, 1)):
         multiply(o)
     for h in range(2):
         got(h, 1 - h, off(h, 2, 1), off(h, 2, 3))
+    for o in ((1, 3), (3, 1), (3, 3)):
+        multiply(o)
     for s in (1, 3):
         for h in range(2):
             far(h, 1 - h, off(h, s, 2))
-    for o in ((1, 2), (3, 2), (2, 1), (2, 3)):
-        multiply(o)
+        multiply((s, 2))
+        multiply((2, s))
     for h in range(2):
         far(h, 1 - h, off(h, 2, 2))
     multiply((2, 2))
@@ -253,7 +256,8 @@
         col_sums = col_sums + stats[i, 0:1, :]
         squares = squares + stats[i, 1:2, :]
         col_max = jnp.maximum(col_max, stats[i, 2:3, :])
-    peak = jnp.max(col_max / col_sums - squares / (col_sums * col_sums), axis=1, keepdims=True)
+    peak = col_max / col_sums - squares / (col_sums * col_sums)
+    peak = jnp.maximum(jnp.maximum(peak[:, :T], peak[:, T:2 * T]), peak[:, 2 * T:])
     peaks[0] = jnp.broadcast_to(peak, (8, T))
     cps = []
     for i, o in enumerate(OFFS[1:]):
@@ -262,14 +266,14 @@
     inverse = 1.0 / col_sums
     nodes = float(8 * ROWS)
     out_ref[...] = acc[...] * inverse * nodes
+    for cp in sends:
+        cp.wait_send()
     for cp in cps:
         cp.wait_recv()
     best = peaks[0]
     for i in range(1, 16):
         best = jnp.maximum(best, peaks[i])
     chaos_ref[0, 0] = jnp.max(best) * nodes
-    for cp in sends:
-        cp.wait_send()
 
 
 def body(transition, tile_pattern, kept_tiles):

time: 123 us -> 123 us (level)
  no operation moved by 1% of the time
where the time goes in v5:
time: 123 us; the launch traced here: 122 us
  Pallas kernels  119 us (97%)
  between operations  2.33 us (2%)
  local copies, waits for them, and re-layouts  1.41 us (1%)
    pallas_call x1, Pallas kernels, body(): pl.pallas_call(main_kernel, out_shape=(jax.ShapeDtypeStruct((ROWS, W), jn...  119 us

profile of v5, /device:TPU:1, one launch (start us, length us, event | category | flops | bytes accessed | tf_op | source)
XLA Modules:
  0.0 122.4 jit_solution(711191399952983620)
XLA Ops:
  0.6 118.7 %shard_map.50 = (f32[1536,384]{1,0:T(8,128)S(1)}, f32[1,1]{1,0:T(1,128)}) custom-call(s32[6,12]{1,0:T(8,128)} %bitcast.5, s32[3,12]{1,0:T(4,128)} %bitcast.6, bf16[12,128,768]{2,1,0:T(8,128)(2,1)} %bitcast.4), custom_call_target="tpu_custom_call" | custom-call | flops 14495514624 | bytes 8388608 | tf_op jit(solution)/shard_map/pallas_call | solution.py:282
  119.3 1.4 %copy.7 = f32[1536,384]{1,0:T(8,128)} copy(f32[1536,384]{1,0:T(8,128)S(1)} %get-tuple-element.8) | data formatting | bytes 4718592

commit v6 on v5

--- a/solution.py
+++ b/solution.py
@@ -30,8 +30,7 @@
         return (((y + dy) % 4) * 2 + (core + dc) % 2, col)
 
     barrier = pltpu.get_barrier_semaphore()
-    others = [plane(*o) for o in sorted(OFFS[1:], key=lambda o: min(o[0], 4 - o[0]) + min(o[1], 4 - o[1]))]
-    others += [line(dy, dc) for dy in range(4) for dc in range(2) if (dy, dc) != (0, 0)]
+    others = [plane(1, 0), plane(3, 0), plane(0, 1), plane(0, 3), line(1, 0), line(3, 0), line(0, 1)]
     for d in others:
         pl.semaphore_signal(barrier, inc=1, device_id=d, device_id_type=MESH)
     loads = [

time: 123 us -> 122 us (level)
  no operation moved by 1% of the time
where the time goes in v6:
time: 122 us
  Pallas kernels  118 us (97%)
  between operations  2.33 us (2%)
  local copies, waits for them, and re-layouts  1.41 us (1%)
    pallas_call x1, Pallas kernels, body(): pl.pallas_call(main_kernel, out_shape=(jax.ShapeDtypeStruct((ROWS, W), jn...  118 us

profile of v6, /device:TPU:1, one launch (start us, length us, event | category | flops | bytes accessed | tf_op | source)
XLA Modules:
  0.0 122.2 jit_solution(8422396986954437643)
XLA Ops:
  0.6 118.4 %shard_map.50 = (f32[1536,384]{1,0:T(8,128)S(1)}, f32[1,1]{1,0:T(1,128)}) custom-call(s32[6,12]{1,0:T(8,128)} %bitcast.5, s32[3,12]{1,0:T(4,128)} %bitcast.6, bf16[12,128,768]{2,1,0:T(8,128)(2,1)} %bitcast.4), custom_call_target="tpu_custom_call" | custom-call | flops 14495514624 | bytes 8388608 | tf_op jit(solution)/shard_map/pallas_call | solution.py:281
  119.1 1.4 %copy.7 = f32[1536,384]{1,0:T(8,128)} copy(f32[1536,384]{1,0:T(8,128)S(1)} %get-tuple-element.8) | data formatting | bytes 4718592
